TPU v7x, 32 devices: a whole 2x2x4 slice. The times are simulated.
32 devices in a mesh: row: 8 (over y, x, core), col: 4 (over z).
Axes of the slice: x: 2, y: 2, z: 4, core: 2. Of those that a mesh axis runs over, the one named last changes fastest.
Arguments:
- embeddings: bfloat16 [4096, 256], P(('row', 'col')), may hold values from -6 to 6
- cotangent: bfloat16 [4096, 256], P(('row', 'col')), may hold values from -6 to 6
- weight: bfloat16 [256, 256], replicated, may hold values from -0.375 to 0.375
- tiles: bfloat16 [32, 128, 128, 128], P(('row', 'col')), may hold values from -0.078125 to 0.078125
- tile_dst: int32 [32, 128], P(('row', 'col')), may hold values from 0 to 3
- tile_src: int32 [32, 128], P(('row', 'col')), may hold values from 0 to 7
- tile_count: int32 [32], P(('row', 'col')), may hold values from 1 to 128, as said below
Outputs:
- output: bfloat16 [4096, 256], P(('row', 'col'))
- grad_embeddings: bfloat16 [4096, 256], P(('row', 'col'))
- grad_weight: float32 [256, 256], replicated
Inputs may be any that keep to these rules, and one draw needn't show every extreme that they name: `tile_count`: at least one device has exactly 128 live slots.
All inputs are finite; a program needn't handle non-finite values.
Results may differ from a plain program's by a relative error of at most 0.012.
Values may be sent and summed in bfloat16 or wider, within the bound.
A program may use at most 128 MiB of HBM per device.

v0:
```python
import math
import jax
import jax.numpy as jnp
from jax import lax
from jax.sharding import PartitionSpec as P


def shards(embeddings, cotangent, weight, tiles, tile_dst, tile_src, tile_count):
    highest = lax.Precision.HIGHEST
    block_rows = embeddings.shape[0]
    feature_width = embeddings.shape[1]
    row_count = lax.axis_size("row")
    column_count = lax.axis_size("col")
    local_tiles = tiles[0]
    dest_ids = tile_dst[0]
    source_ids = tile_src[0]
    slot_ids = jnp.arange(local_tiles.shape[0], dtype=jnp.int32)
    alive_slots = (slot_ids < tile_count[0]).astype(jnp.float32)
    dest_onehot = (dest_ids[:, None] == jnp.arange(column_count, dtype=jnp.int32)[None, :]).astype(
        jnp.float32
    ) * alive_slots[:, None]
    source_onehot = (source_ids[:, None] == jnp.arange(row_count, dtype=jnp.int32)[None, :]).astype(
        jnp.float32
    ) * alive_slots[:, None]
    gathered = lax.all_gather(embeddings, "row", axis=0, tiled=True).reshape(
        row_count, block_rows, feature_width
    )
    chosen = jnp.take(gathered, source_ids, axis=0)
    products = jnp.einsum("tij,tjd->tid", local_tiles, chosen, preferred_element_type=jnp.float32)
    partial_value = jnp.einsum("tc,tid->cid", dest_onehot, products, precision=highest)
    partial_rounded = partial_value.astype(jnp.bfloat16).reshape(
        column_count * block_rows, feature_width
    )
    summed = lax.psum_scatter(
        partial_rounded.astype(jnp.float32).astype(jnp.bfloat16),
        "col",
        scatter_dimension=0,
        tiled=True,
    ).astype(jnp.float32)
    hidden = summed.astype(jnp.bfloat16)
    output = jnp.dot(hidden, weight, preferred_element_type=jnp.float32).astype(jnp.bfloat16)
    user_count = block_rows * row_count * column_count
    scale_factor = 1.0 / math.sqrt(user_count)
    contract_rows = (((0,), (0,)), ((), ()))
    contract_cols = (((1,), (1,)), ((), ()))
    grad_hidden = lax.dot_general(
        cotangent, weight, contract_cols, preferred_element_type=jnp.float32
    ).astype(jnp.bfloat16)
    grad_group = lax.all_gather(grad_hidden, "col", axis=0, tiled=True)
    weight_term = lax.dot_general(
        summed, cotangent.astype(jnp.float32), contract_rows, precision=highest
    )
    grad_weight = lax.psum(weight_term, ("row", "col")) * scale_factor
    dest_rows = grad_group.reshape(column_count, block_rows, feature_width)
    picked = jnp.take(dest_rows, dest_ids, axis=0)
    back_products = jnp.einsum(
        "tji,tjd->tid", local_tiles, picked, preferred_element_type=jnp.float32
    )
    back_partial = jnp.einsum("tr,tid->rid", source_onehot, back_products, precision=highest)
    back_rounded = lax.optimization_barrier(back_partial.astype(jnp.bfloat16)).astype(jnp.float32)
    back_summed = lax.psum_scatter(
        back_rounded.reshape(row_count * block_rows, feature_width).astype(jnp.bfloat16),
        "row",
        scatter_dimension=0,
        tiled=True,
    )
    return (output, back_summed, grad_weight)


def solution(mesh):
    in_specs = (
        P(("row", "col"), None),
        P(("row", "col"), None),
        P(),
        P(("row", "col"), None, None, None),
        P(("row", "col"), None),
        P(("row", "col"), None),
        P(("row", "col")),
    )
    out_specs = (P(("row", "col"), None), P(("row", "col"), None), P())
    return jax.shard_map(shards, mesh=mesh, in_specs=in_specs, out_specs=out_specs, check_vma=False)
```

profile of v0, /device:TPU:0, one launch (start us, length us, event | category | flops | bytes accessed | tf_op | source)
XLA Modules:
  0.0 260.4 jit_solution(8117860961400061152)
XLA Ops:
  8.0 0.0 copy-start
  8.0 0.0 reduce-scatter.3.cloned.1.call-start
  8.1 0.7 fusion.30
  8.7 0.7 compare_and_fusion.1
  9.4 11.6 %all_gather.6 = bf16[1024,256]{1,0:T(8,128)(2,1)S(1)} all-gather(bf16[128,256]{1,0:T(8,128)(2,1)} %param.7), channel_id=1, replica_groups=mesh['row'=8,'col'=4] {'row'}, dimensions={0}, use_global_device_ids=true | all-gather | bytes 589824 | tf_op jit(solution)/shard_map/all_gather | solution.py:25
  21.0 6.5 %gather_fusion = bf16[128,128,256]{2,1,0:T(8,128)(2,1)} fusion(bf16[8,128,256]{2,1,0:T(8,128)(2,1)S(1)} %bitcast.46, s32[1024]{0:T(1024)S(1)} %pad_clamp_fusion.1), kind=kCustom, calls=%fused_computation | custom fusion | bytes 16777728 | tf_op jit(solution)/shard_map/jit(_take)/gather | solution.py:28
  27.5 13.1 %fusion.6 = f32[128,256,128]{2,1,0:T(8,128)} fusion(bf16[128,128,256]{2,1,0:T(8,128)(2,1)} %gather_fusion, pred[128]{0:T(512)(128)(4,1)S(1)} %compare_and_fusion.1, bf16[1,128,128,128]{3,2,1,0:T(8,128)(2,1)} %param.10), kind=kOutput, calls=%fused_computation.8 | convolution fusion | flops 1077936128 | bytes 29360256 | tf_op jit(solution)/shard_map/tij,tjd->tid/dot_general | solution.py:29
  40.6 0.0 copy-start.3
  40.6 17.7 %copy.12 = f32[128,256,128]{1,0,2:T(8,128)} copy(f32[128,256,128]{2,1,0:T(8,128)} %fusion.6) | data formatting | bytes 33554432 | tf_op jit(solution)/shard_map/tij,tjd->tid/dot_general | solution.py:29
  59.0 0.0 copy-done.3
  59.0 0.0 copy-start.1
  59.0 10.8 %fusion.17 = bf16[4,128,256]{2,0,1:T(4,128)(2,1)S(1)} fusion(f32[128,256,128]{1,0,2:T(8,128)} %copy.12, f32[128]{0:T(128)S(1)} %compare_convert_fusion, s32[128]{0:T(128)S(1)} %bitcast.49), kind=kOutput, calls=%fused_computation.17 | convolution fusion | flops 201458688 | bytes 17040384 | tf_op jit(solution)/shard_map/tc,tid->cid/dot_general | solution.py:30
  69.8 0.7 copy.10
  70.6 0.0 reduce-scatter.3.cloned.1.call-update
  70.6 0.0 all-reduce.2.cloned.1.call-start
  70.7 0.0 copy-done
  70.7 0.0 copy-done.1
  70.7 0.2 convolution_convert_fusion
  70.9 15.5 %all_gather.7 = bf16[512,256]{1,0:T(8,128)(2,1)S(1)} all-gather(bf16[128,256]{1,0:T(8,128)(2,1)S(1)} %convolution_convert_fusion), channel_id=1, replica_groups=mesh['row'=8,'col'=4] {'col'}, dimensions={0}, use_global_device_ids=true | all-gather | bytes 327680 | tf_op jit(solution)/shard_map/all_gather | solution.py:49
  86.4 6.5 %gather_fusion.1 = bf16[128,128,256]{2,1,0:T(8,128)(2,1)} fusion(bf16[4,128,256]{2,1,0:T(8,128)(2,1)S(1)} %bitcast.45, s32[1024]{0:T(1024)S(1)} %pad_clamp_fusion), kind=kCustom, calls=%fused_computation.1 | custom fusion | bytes 16777728 | tf_op jit(solution)/shard_map/jit(_take)/gather | solution.py:55
  92.9 12.8 %fusion.4 = f32[128,256,128]{2,1,0:T(8,128)} fusion(bf16[128,128,256]{2,1,0:T(8,128)(2,1)} %gather_fusion.1, pred[128]{0:T(512)(128)(4,1)S(1)} %compare_and_fusion, bf16[1,128,128,128]{3,2,1,0:T(8,128)(2,1)} %param.10), kind=kOutput, calls=%fused_computation.6 | convolution fusion | flops 1077936128 | bytes 29360256 | tf_op jit(solution)/shard_map/tji,tjd->tid/dot_general | solution.py:56
  105.7 0.0 copy-start.4
  105.7 17.7 %copy.13 = f32[128,256,128]{1,0,2:T(8,128)} copy(f32[128,256,128]{2,1,0:T(8,128)} %fusion.4) | data formatting | bytes 33554432 | tf_op jit(solution)/shard_map/tji,tjd->tid/dot_general | solution.py:56
  123.4 0.0 reduce-scatter.3.cloned.1.call-done
  123.4 1.7 fusion.36
  125.1 0.0 all-reduce.2.cloned.1.call-update
  125.2 0.0 reduce-scatter.5.cloned.1.call-start
  125.2 0.0 copy-done.4
  125.2 0.0 copy-start.2
  125.2 10.8 %fusion.14 = bf16[8,128,256]{2,0,1:T(8,128)(2,1)S(1)} fusion(f32[128,256,128]{1,0,2:T(8,128)} %copy.13, f32[128]{0:T(128)S(1)} %compare_convert_fusion, s32[128]{0:T(128)S(1)} %bitcast.50), kind=kOutput, calls=%fused_computation.16 | convolution fusion | flops 402917376 | bytes 17302528 | tf_op jit(solution)/shard_map/tr,tid->rid/dot_general | solution.py:59
  136.1 0.9 copy.11
  137.0 0.0 reduce-scatter.5.cloned.1.call-update
  137.0 0.0 copy-done.2
  137.0 0.8 convolution_convert_fusion.1
  137.8 113.4 %all-reduce.2.cloned.1.call-done = f32[256,256]{1,0:T(8,128)} async-done(((f32[256,256]{1,0:T(8,128)}), f32[256,256]{1,0:T(8,128)}) %all-reduce.2.cloned.1.call-update) | async-done | bytes 262160 | tf_op jit(solution)/shard_map/psum | solution.py:53
  251.3 1.7 broadcast_multiply_fusion
  252.9 0.0 reduce-scatter.5.cloned.1.call-done
  (5 shorter events, 0.0 us)
Async XLA Ops:
  8.0 62.7 %copy-start = (bf16[256,256]{1,0:T(8,128)(2,1)S(1)}, bf16[256,256]{1,0:T(8,128)(2,1)}, u32[]{:S(2)}) copy-start(bf16[256,256]{1,0:T(8,128)(2,1)} %param.9) | copy-start | bytes 393220
  8.0 115.4 %reduce-scatter.3.cloned.1.call-start = ((), (), s32[]{:S(2)}) async-start(), calls=%async_computation.2 | async-start | bytes 327680 | tf_op jit(solution)/shard_map/reduce_scatter | solution.py:34
  40.6 18.4 %copy-start.3 = (s32[1,128]{1,0:T(1,128)S(1)}, s32[1,128]{1,0:T(1,128)}, u32[]{:S(2)}) copy-start(s32[1,128]{1,0:T(1,128)} %param.11) | copy-start | bytes 1540
  59.0 11.7 %copy-start.1 = (bf16[128,256]{1,0:T(8,128)(2,1)S(1)}, bf16[128,256]{1,0:T(8,128)(2,1)}, u32[]{:S(2)}) copy-start(bf16[128,256]{1,0:T(8,128)(2,1)} %param.8) | copy-start | bytes 196612
  70.6 180.7 %all-reduce.2.cloned.1.call-start = ((), (), s32[]{:S(2)}) async-start(), calls=%async_computation.4 | async-start | bytes 524288 | tf_op jit(solution)/shard_map/psum | solution.py:53
  105.7 19.5 %copy-start.4 = (s32[1,128]{1,0:T(1,128)S(1)}, s32[1,128]{1,0:T(1,128)}, u32[]{:S(2)}) copy-start(s32[1,128]{1,0:T(1,128)} %param.12) | copy-start | bytes 1540
  125.2 127.8 %reduce-scatter.5.cloned.1.call-start = ((), (), s32[]{:S(2)}) async-start(), calls=%async_computation.3 | async-start | bytes 589824 | tf_op jit(solution)/shard_map/reduce_scatter | solution.py:61
  125.2 11.8 %copy-start.2 = (bf16[128,256]{1,0:T(8,128)(2,1)S(1)}, bf16[128,256]{1,0:T(8,128)(2,1)}, u32[]{:S(2)}) copy-start(bf16[128,256]{1,0:T(8,128)(2,1)} %reduce-scatter.3.cloned.1.call-done) | copy-start | bytes 196612
Sparse Core Ops, SparseCore 0:
  70.7 20.6 reduce-scatter.2
  125.3 125.9 all-reduce.1
Sparse Core Ops, SparseCore 1:
  137.1 34.8 reduce-scatter.4
where the time goes:
time: 261 us; the launch traced here: 260 us
  waiting for transfers between devices  113 us (43%)
  matrix products  50.3 us (19%)
  local copies, waits for them, and re-layouts  50 us (19%)
  blocking collectives  27.1 us (10%)
  between operations  16.3 us (6%)
  other arithmetic  3.05 us (1%)
    psum x1, waiting for transfers between devices, shards(): grad_weight = lax.psum(weight_term, ('row', 'col')) * scale_factor  113 us
    dot_general x1, local copies, waits for them, and re-layouts, shards(): jnp.einsum('tij,tjd->tid', local_tiles, chosen, preferred_element_type=jn...  17.7 us
    dot_general x1, local copies, waits for them, and re-layouts, shards(): jnp.einsum('tji,tjd->tid', local_tiles, picked, preferred_element_type=jn...  17.7 us
    all_gather x1, blocking collectives, shards(): grad_group = lax.all_gather(grad_hidden, 'col', axis=0, tiled=True)  15.5 us
    dot_general x1, matrix products, shards(): jnp.einsum('tij,tjd->tid', local_tiles, chosen, preferred_element_type=jn...  13.1 us
    dot_general x1, matrix products, shards(): jnp.einsum('tji,tjd->tid', local_tiles, picked, preferred_element_type=jn...  12.8 us
    all_gather x1, blocking collectives, shards(): lax.all_gather(embeddings, 'row', axis=0, tiled=True)  11.6 us
    dot_general x1, matrix products, shards(): jnp.einsum('tc,tid->cid', dest_onehot, products, precision=highest)  10.8 us
  transfers between devices with their start and end apart: 3, of which 1 were waited for; matrix products, arithmetic and copies ran while one was open for 20% of the time, Pallas kernels for 0%

commit v1 on v0

--- a/solution.py
+++ b/solution.py
@@ -3,6 +3,21 @@
 import jax.numpy as jnp
 from jax import lax
 from jax.sharding import PartitionSpec as P
+
+
+def draft_area_all(packet):
+    dev_axis = "col"
+    axis_len = lax.axis_size(dev_axis)
+    found = [packet]
+    ii = 0
+    while ii < axis_len - 1:
+        found.append(
+            lax.ppermute(found[-1], dev_axis, [(m, (m + 1) % axis_len) for m in range(axis_len)])
+        )
+        ii += 1
+    r1 = jnp.concatenate(found[::-1], 0)
+    piece_next = lax.axis_index(dev_axis)
+    return jnp.roll(r1, (piece_next + 1) * packet.shape[0], 0)
 
 
 def shards(embeddings, cotangent, weight, tiles, tile_dst, tile_src, tile_count):
@@ -46,7 +61,7 @@
     grad_hidden = lax.dot_general(
         cotangent, weight, contract_cols, preferred_element_type=jnp.float32
     ).astype(jnp.bfloat16)
-    grad_group = lax.all_gather(grad_hidden, "col", axis=0, tiled=True)
+    grad_group = draft_area_all(grad_hidden)
     weight_term = lax.dot_general(
         summed, cotangent.astype(jnp.float32), contract_rows, precision=highest
     )

time: 261 us -> 259 us (level)
  blocking collectives: 27.1 us -> 10.2 us
  waiting for transfers between devices: 113 us -> 122 us
  starting transfers between devices: 0.12 us -> 4.87 us
    all_gather x1 -> x0, blocking collectives: 15.5 us -> none  [shards(): grad_group = lax.all_gather(grad_hidden, 'col', axis=0, tiled=True)]
    ppermute x0 -> x3, waiting for transfers between devices: none -> 11.5 us  [draft_area_all(): lax.ppermute(found[-1], dev_axis, [(m, (m + 1) % axis_len) for m in range...]
    ppermute x0 -> x3, starting transfers between devices: none -> 4.75 us  [draft_area_all(): lax.ppermute(found[-1], dev_axis, [(m, (m + 1) % axis_len) for m in range...]
    psum x1, waiting for transfers between devices: 113 us -> 110 us  [shards(): grad_weight = lax.psum(weight_term, ('row', 'col')) * scale_factor]
  transfers between devices with their start and end apart: 3 -> 6, of which waited for: 1 -> 3; matrix products, arithmetic and copies ran while one was open for 20% -> 39% of each run, Pallas kernels for 0% -> 0%
where the time goes in v1:
time: 259 us; the launch traced here: 258 us
  waiting for transfers between devices  122 us (47%)
  matrix products  51.3 us (20%)
  local copies, waits for them, and re-layouts  51.1 us (20%)
  between operations  16.3 us (6%)
  blocking collectives  10.2 us (4%)
  starting transfers between devices  4.87 us (2%)
  other arithmetic  3.01 us (1%)
    psum x1, waiting for transfers between devices, shards(): grad_weight = lax.psum(weight_term, ('row', 'col')) * scale_factor  110 us
    dot_general x1, local copies, waits for them, and re-layouts, shards(): jnp.einsum('tji,tjd->tid', local_tiles, picked, preferred_element_type=jn...  17.7 us
    dot_general x1, local copies, waits for them, and re-layouts, shards(): jnp.einsum('tij,tjd->tid', local_tiles, chosen, preferred_element_type=jn...  17.7 us
    dot_general x1, matrix products, shards(): jnp.einsum('tij,tjd->tid', local_tiles, chosen, preferred_element_type=jn...  13.2 us
    dot_general x1, matrix products, shards(): jnp.einsum('tji,tjd->tid', local_tiles, picked, preferred_element_type=jn...  12.8 us
    ppermute x3, waiting for transfers between devices, draft_area_all(): lax.ppermute(found[-1], dev_axis, [(m, (m + 1) % axis_len) for m in range...  11.5 us
    dot_general x1, matrix products, shards(): jnp.einsum('tr,tid->rid', source_onehot, back_products, precision=highest)  10.8 us
    dot_general x1, matrix products, shards(): jnp.einsum('tc,tid->cid', dest_onehot, products, precision=highest)  10.8 us
  transfers between devices with their start and end apart: 6, of which 3 were waited for; matrix products, arithmetic and copies ran while one was open for 39% of the time, Pallas kernels for 0%

profile of v1, /device:TPU:0, one launch (start us, length us, event | category | flops | bytes accessed | tf_op | source)
XLA Modules:
  0.0 258.4 jit_solution(18061226589122918239)
XLA Ops:
  8.0 0.0 copy-start
  8.0 0.0 reduce-scatter.3.cloned.1.call-start
  8.1 0.8 copy-done
  8.9 1.0 convolution_convert_fusion
  9.9 3.1 %collective-permute-start = (bf16[128,256]{1,0:T(8,128)(2,1)S(1)}, bf16[128,256]{1,0:T(8,128)(2,1)S(1)}, u32[]{:S(2)}, u32[]{:S(2)}) collective-permute-start(bf16[128,256]{1,0:T(8,128)(2,1)S(1)} %convolution_convert_fusion), channel_id=1, source_target_pairs={{0,1},{1,2},{2,3},{3,0},{4,5},{5,6},{6,7},{7,4},{8,9},{9,10},{10,1... | collective-permute-start | bytes 196616 | tf_op jit(solution)/shard_map/ppermute | solution.py:15
  13.0 0.7 fusion.30
  13.7 0.7 compare_and_fusion.1
  15.0 10.2 %all_gather.3 = bf16[1024,256]{1,0:T(8,128)(2,1)S(1)} all-gather(bf16[128,256]{1,0:T(8,128)(2,1)} %param.7), channel_id=1, replica_groups=mesh['row'=8,'col'=4] {'row'}, dimensions={0}, use_global_device_ids=true | all-gather | bytes 589824 | tf_op jit(solution)/shard_map/all_gather | solution.py:40
  25.2 6.5 %gather_fusion = bf16[128,128,256]{2,1,0:T(8,128)(2,1)} fusion(bf16[8,128,256]{2,1,0:T(8,128)(2,1)S(1)} %bitcast.46, s32[1024]{0:T(1024)S(1)} %pad_clamp_fusion.1), kind=kCustom, calls=%fused_computation | custom fusion | bytes 16777728 | tf_op jit(solution)/shard_map/jit(_take)/gather | solution.py:43
  31.7 13.2 %fusion.6 = f32[128,256,128]{2,1,0:T(8,128)} fusion(bf16[128,128,256]{2,1,0:T(8,128)(2,1)} %gather_fusion, pred[128]{0:T(512)(128)(4,1)S(1)} %compare_and_fusion.1, bf16[1,128,128,128]{3,2,1,0:T(8,128)(2,1)} %param.10), kind=kOutput, calls=%fused_computation.8 | convolution fusion | flops 1077936128 | bytes 29360256 | tf_op jit(solution)/shard_map/tij,tjd->tid/dot_general | solution.py:44
  44.9 0.0 copy-start.3
  44.9 17.7 %copy.12 = f32[128,256,128]{1,0,2:T(8,128)} copy(f32[128,256,128]{2,1,0:T(8,128)} %fusion.6) | data formatting | bytes 33554432 | tf_op jit(solution)/shard_map/tij,tjd->tid/dot_general | solution.py:44
  62.6 0.0 copy-done.3
  62.6 10.8 %fusion.17 = bf16[4,128,256]{2,0,1:T(4,128)(2,1)S(1)} fusion(f32[128,256,128]{1,0,2:T(8,128)} %copy.12, f32[128]{0:T(128)S(1)} %compare_convert_fusion, s32[128]{0:T(128)S(1)} %bitcast.49), kind=kOutput, calls=%fused_computation.17 | convolution fusion | flops 201458688 | bytes 17040384 | tf_op jit(solution)/shard_map/tc,tid->cid/dot_general | solution.py:45
  73.4 0.7 copy.10
  74.2 0.0 reduce-scatter.3.cloned.1.call-update
  74.2 0.0 all-reduce.2.cloned.1.call-start
  74.2 0.0 collective-permute-done
  74.2 1.7 collective-permute-start.1
  75.9 4.6 %collective-permute-done.1 = bf16[128,256]{1,0:T(8,128)(2,1)S(1)} collective-permute-done((bf16[128,256]{1,0:T(8,128)(2,1)S(1)}, bf16[128,256]{1,0:T(8,128)(2,1)S(1)}, u32[]{:S(2)}, u32[]{:S(2)}) %collective-permute-start.1) | collective-permute-done | bytes 65568 | tf_op jit(solution)/shard_map/ppermute | solution.py:15
  80.5 0.0 collective-permute-start.2
  80.5 7.0 %collective-permute-done.2 = bf16[128,256]{1,0:T(8,128)(2,1)S(1)} collective-permute-done((bf16[128,256]{1,0:T(8,128)(2,1)S(1)}, bf16[128,256]{1,0:T(8,128)(2,1)S(1)}, u32[]{:S(2)}, u32[]{:S(2)}) %collective-permute-start.2) | collective-permute-done | bytes 65568 | tf_op jit(solution)/shard_map/ppermute | solution.py:15
  87.6 6.5 %gather_fusion.1 = bf16[128,128,256]{2,1,0:T(8,128)(2,1)} fusion(bf16[4,128,256]{2,1,0:T(8,128)(2,1)S(1)} %bitcast.45, s32[1024]{0:T(1024)S(1)} %pad_clamp_fusion), kind=kCustom, calls=%fused_computation.1 | custom fusion | bytes 16777728 | tf_op jit(solution)/shard_map/jit(_take)/gather | solution.py:70
  94.1 12.8 %fusion.4 = f32[128,256,128]{2,1,0:T(8,128)} fusion(bf16[128,128,256]{2,1,0:T(8,128)(2,1)} %gather_fusion.1, pred[128]{0:T(512)(128)(4,1)S(1)} %compare_and_fusion, bf16[1,128,128,128]{3,2,1,0:T(8,128)(2,1)} %param.10), kind=kOutput, calls=%fused_computation.6 | convolution fusion | flops 1077936128 | bytes 29360256 | tf_op jit(solution)/shard_map/tji,tjd->tid/dot_general | solution.py:71
  107.0 0.0 copy-start.1
  107.0 0.0 copy-start.4
  107.0 17.7 %copy.13 = f32[128,256,128]{1,0,2:T(8,128)} copy(f32[128,256,128]{2,1,0:T(8,128)} %fusion.4) | data formatting | bytes 33554432 | tf_op jit(solution)/shard_map/tji,tjd->tid/dot_general | solution.py:71
  124.7 0.0 reduce-scatter.3.cloned.1.call-done
  124.7 0.0 copy-done.1
  124.7 1.8 fusion.36
  126.5 0.0 all-reduce.2.cloned.1.call-update
  126.5 0.0 reduce-scatter.5.cloned.1.call-start
  126.5 0.0 copy-done.4
  126.5 0.0 copy-start.2
  126.6 10.8 %fusion.14 = bf16[8,128,256]{2,0,1:T(8,128)(2,1)S(1)} fusion(f32[128,256,128]{1,0,2:T(8,128)} %copy.13, f32[128]{0:T(128)S(1)} %compare_convert_fusion, s32[128]{0:T(128)S(1)} %bitcast.50), kind=kOutput, calls=%fused_computation.16 | convolution fusion | flops 402917376 | bytes 17302528 | tf_op jit(solution)/shard_map/tr,tid->rid/dot_general | solution.py:74
  137.4 0.9 copy.11
  138.3 0.0 reduce-scatter.5.cloned.1.call-update
  138.3 0.0 copy-done.2
  138.3 0.8 convolution_convert_fusion.1
  139.1 110.2 %all-reduce.2.cloned.1.call-done = f32[256,256]{1,0:T(8,128)} async-done(((f32[256,256]{1,0:T(8,128)}), f32[256,256]{1,0:T(8,128)}) %all-reduce.2.cloned.1.call-update) | async-done | bytes 262160 | tf_op jit(solution)/shard_map/psum | solution.py:68
  249.3 1.7 broadcast_multiply_fusion
  251.0 0.0 reduce-scatter.5.cloned.1.call-done
  (14 shorter events, 0.1 us)
Async XLA Ops:
  8.0 0.9 copy-start
  8.0 116.7 %reduce-scatter.3.cloned.1.call-start = ((), (), s32[]{:S(2)}) async-start(), calls=%async_computation.2 | async-start | bytes 327680 | tf_op jit(solution)/shard_map/reduce_scatter | solution.py:49
  9.9 64.3 %collective-permute-start = (bf16[128,256]{1,0:T(8,128)(2,1)S(1)}, bf16[128,256]{1,0:T(8,128)(2,1)S(1)}, u32[]{:S(2)}, u32[]{:S(2)}) collective-permute-start(bf16[128,256]{1,0:T(8,128)(2,1)S(1)} %convolution_convert_fusion), channel_id=1, source_target_pairs={{0,1},{1,2},{2,3},{3,0},{4,5},{5,6},{6,7},{7,4},{8,9},{9,10},{10,1... | collective-permute-start | bytes 196616 | tf_op jit(solution)/shard_map/ppermute | solution.py:15
  44.9 17.7 %copy-start.3 = (s32[1,128]{1,0:T(1,128)S(1)}, s32[1,128]{1,0:T(1,128)}, u32[]{:S(2)}) copy-start(s32[1,128]{1,0:T(1,128)} %param.11) | copy-start | bytes 1540
  74.2 175.1 %all-reduce.2.cloned.1.call-start = ((), (), s32[]{:S(2)}) async-start(), calls=%async_computation.4 | async-start | bytes 524288 | tf_op jit(solution)/shard_map/psum | solution.py:68
  74.2 6.2 %collective-permute-start.1 = (bf16[128,256]{1,0:T(8,128)(2,1)S(1)}, bf16[128,256]{1,0:T(8,128)(2,1)S(1)}, u32[]{:S(2)}, u32[]{:S(2)}) collective-permute-start(bf16[128,256]{1,0:T(8,128)(2,1)S(1)} %collective-permute-done), channel_id=1, source_target_pairs={{0,1},{1,2},{2,3},{3,0},{4,5},{5,6},{6,7},{7,4},{8,9},{9,10},{10,1... | collective-permute-start | bytes 196616 | tf_op jit(solution)/shard_map/ppermute | solution.py:15
  80.5 7.0 %collective-permute-start.2 = (bf16[128,256]{1,0:T(8,128)(2,1)S(1)}, bf16[128,256]{1,0:T(8,128)(2,1)S(1)}, u32[]{:S(2)}, u32[]{:S(2)}) collective-permute-start(bf16[128,256]{1,0:T(8,128)(2,1)S(1)} %collective-permute-done.1), channel_id=1, source_target_pairs={{0,1},{1,2},{2,3},{3,0},{4,5},{5,6},{6,7},{7,4},{8,9},{9,10},{10,1... | collective-permute-start | bytes 196616 | tf_op jit(solution)/shard_map/ppermute | solution.py:15
  107.0 17.7 %copy-start.1 = (bf16[128,256]{1,0:T(8,128)(2,1)S(1)}, bf16[128,256]{1,0:T(8,128)(2,1)}, u32[]{:S(2)}) copy-start(bf16[128,256]{1,0:T(8,128)(2,1)} %param.8) | copy-start | bytes 196612
  107.0 19.6 %copy-start.4 = (s32[1,128]{1,0:T(1,128)S(1)}, s32[1,128]{1,0:T(1,128)}, u32[]{:S(2)}) copy-start(s32[1,128]{1,0:T(1,128)} %param.12) | copy-start | bytes 1540
  126.5 124.5 %reduce-scatter.5.cloned.1.call-start = ((), (), s32[]{:S(2)}) async-start(), calls=%async_computation.3 | async-start | bytes 589824 | tf_op jit(solution)/shard_map/reduce_scatter | solution.py:76
  126.5 11.8 %copy-start.2 = (bf16[128,256]{1,0:T(8,128)(2,1)S(1)}, bf16[128,256]{1,0:T(8,128)(2,1)}, u32[]{:S(2)}) copy-start(bf16[128,256]{1,0:T(8,128)(2,1)} %reduce-scatter.3.cloned.1.call-done) | copy-start | bytes 196612
Sparse Core Ops, SparseCore 0:
  74.3 19.1 reduce-scatter.2
  126.6 122.6 all-reduce.1
Sparse Core Ops, SparseCore 1:
  138.4 31.6 reduce-scatter.4
